TPU v7x, 256 devices: a whole 4x4x8 slice. The times are simulated.
256 devices in a mesh: grp: 4 (over z_hi), wr: 64 (over y, x, z_lo, core).
Axes of the slice: x: 4, y: 4, z: 8 (z_hi: 4, z_lo: 2; z = z_hi * 2 + z_lo), core: 2. Of those that a mesh axis runs over, the one named last changes fastest.
Arguments:
- snapshots: float32 [256, 1048576], P('wr', 'grp'), may hold values from -1300 to 1300
Outputs:
- basis: float32 [256, 1048576], P(None, ('grp', 'wr'))
- r_scaled: float32 [256, 256], P(None, 'wr')
All inputs are finite; a program needn't handle non-finite values.
Results may differ from a plain program's by a relative error of at most 0.000073.
Values sent between devices are 32-bit elements; how exact they have to be, the bound alone decides.
A program may use at most 64 MiB of HBM per device.

v0:
```python
import jax
import jax.numpy as jnp
from jax import lax
from jax.sharding import PartitionSpec as P


def partner(value, axis, stride):
    return lax.ppermute(value, axis, [(i, i ^ 1 << stride) for i in range(lax.axis_size(axis))])


def products(left, right):
    return lax.dot_general(
        left,
        right,
        (((1,), (1,)), ((), ())),
        precision=lax.Precision.HIGHEST,
        preferred_element_type=jnp.float32,
    )


def writer_levels(gram):
    for bit in range(lax.axis_size("wr").bit_length() - 1):
        gram = gram + partner(gram, "wr", bit)
    return gram


def group_levels(gram):
    for bit in range(lax.axis_size("grp").bit_length() - 1):
        gram = gram + partner(gram, "grp", bit)
    return gram


def body(snapshots):
    regrouped = lax.all_to_all(snapshots, "wr", split_axis=1, concat_axis=0, tiled=True)
    local_gram = products(regrouped, regrouped)
    total = writer_levels(group_levels(local_gram))
    lower = jnp.linalg.cholesky(total)
    cell_count = regrouped.shape[1] * lax.axis_size("grp") * lax.axis_size("wr")
    scale = jnp.sqrt(jnp.float32(cell_count))
    solved = lax.linalg.triangular_solve(lower, regrouped, left_side=True, lower=True)
    width = lower.shape[0] // lax.axis_size("wr")
    start = lax.axis_index("wr") * width
    columns = lax.dynamic_slice_in_dim(lower.T, start, width, 1)
    return (solved * scale, columns / scale)


def solution(mesh):
    placed = (P("wr", "grp"),)
    return jax.shard_map(
        body,
        mesh=mesh,
        in_specs=placed,
        out_specs=(P(None, ("grp", "wr")), P(None, "wr")),
        check_vma=False,
    )
```

profile of v0, /device:TPU:1, one launch (start us, length us, event | category | flops | bytes accessed | tf_op | source)
XLA Modules:
  0.0 221.2 jit_solution(17695006843212439441)
XLA Ops:
  0.6 62.5 %all_to_all.19 = f32[4,64,4096]{2,0,1:T(4,128)} all-to-all(f32[4,64,4096]{2,0,1:T(4,128)} %bitcast.40), channel_id=1, replica_groups=mesh['grp'=4,'wr'=64] {'wr'}, dimensions={1} | all-to-all | bytes 8388608 | tf_op jit(solution)/shard_map/all_to_all | solution.py:34
  63.1 5.3 %all_to_all.17 = f32[256,4096]{1,0:T(8,128)} reshape(f32[64,4,4096]{2,1,0:T(4,128)} %bitcast.38) | data formatting | bytes 8388608 | tf_op jit(solution)/shard_map/all_to_all | solution.py:34
  68.4 11.9 %fusion.10 = f32[256,256]{0,1:T(8,128)S(1)} fusion(f32[256,4096]{1,0:T(8,128)} %all_to_all.17), kind=kOutput, calls=%fused_computation.31 | convolution fusion | flops 3221225472 | bytes 4456448 | tf_op jit(solution)/shard_map/dot_general | solution.py:12
  80.3 3.1 %collective-permute-start = (f32[256,256]{0,1:T(8,128)S(1)}, f32[256,256]{0,1:T(8,128)S(1)}, u32[]{:S(2)}, u32[]{:S(2)}) collective-permute-start(f32[256,256]{0,1:T(8,128)S(1)} %fusion.10), channel_id=1, source_target_pairs={{0,64},{64,0},{128,192},{192,128},{1,65},{65,1},{129,193},{193,129... | collective-permute-start | bytes 786440 | tf_op jit(solution)/shard_map/ppermute | solution.py:8
  83.4 10.9 %collective-permute-done = f32[256,256]{0,1:T(8,128)S(1)} collective-permute-done((f32[256,256]{0,1:T(8,128)S(1)}, f32[256,256]{0,1:T(8,128)S(1)}, u32[]{:S(2)}, u32[]{:S(2)}) %collective-permute-start) | collective-permute-done | bytes 262176 | tf_op jit(solution)/shard_map/ppermute | solution.py:8
  94.3 5.4 %collective-permute-start.1 = (f32[256,256]{0,1:T(8,128)S(1)}, f32[256,256]{0,1:T(8,128)S(1)}, u32[]{:S(2)}, u32[]{:S(2)}) collective-permute-start(f32[256,256]{0,1:T(8,128)S(1)} %add.49), channel_id=1, source_target_pairs={{0,128},{64,192},{128,0},{192,64},{1,129},{65,193},{129,1},{193,65... | collective-permute-start | bytes 786440 | tf_op jit(solution)/shard_map/ppermute | solution.py:8
  99.8 11.6 %collective-permute-done.1 = f32[256,256]{0,1:T(8,128)S(1)} collective-permute-done((f32[256,256]{0,1:T(8,128)S(1)}, f32[256,256]{0,1:T(8,128)S(1)}, u32[]{:S(2)}, u32[]{:S(2)}) %collective-permute-start.1) | collective-permute-done | bytes 262176 | tf_op jit(solution)/shard_map/ppermute | solution.py:8
  111.4 1.4 collective-permute-start.2
  112.8 1.2 collective-permute-done.2
  114.0 0.1 collective-permute-start.3
  114.1 7.5 %collective-permute-done.3 = f32[256,256]{0,1:T(8,128)S(1)} collective-permute-done((f32[256,256]{0,1:T(8,128)S(1)}, f32[256,256]{0,1:T(8,128)S(1)}, u32[]{:S(2)}, u32[]{:S(2)}) %collective-permute-start.3) | collective-permute-done | bytes 262176 | tf_op jit(solution)/shard_map/ppermute | solution.py:8
  121.7 0.1 collective-permute-start.4
  121.8 6.6 %collective-permute-done.4 = f32[256,256]{0,1:T(8,128)S(1)} collective-permute-done((f32[256,256]{0,1:T(8,128)S(1)}, f32[256,256]{0,1:T(8,128)S(1)}, u32[]{:S(2)}, u32[]{:S(2)}) %collective-permute-start.4) | collective-permute-done | bytes 262176 | tf_op jit(solution)/shard_map/ppermute | solution.py:8
  128.4 1.8 collective-permute-start.5
  130.2 5.4 %collective-permute-done.5 = f32[256,256]{0,1:T(8,128)S(1)} collective-permute-done((f32[256,256]{0,1:T(8,128)S(1)}, f32[256,256]{0,1:T(8,128)S(1)}, u32[]{:S(2)}, u32[]{:S(2)}) %collective-permute-start.5) | collective-permute-done | bytes 262176 | tf_op jit(solution)/shard_map/ppermute | solution.py:8
  135.7 0.4 collective-permute-start.6
  136.1 4.9 %collective-permute-done.6 = f32[256,256]{0,1:T(8,128)S(1)} collective-permute-done((f32[256,256]{0,1:T(8,128)S(1)}, f32[256,256]{0,1:T(8,128)S(1)}, u32[]{:S(2)}, u32[]{:S(2)}) %collective-permute-start.6) | collective-permute-done | bytes 262176 | tf_op jit(solution)/shard_map/ppermute | solution.py:8
  141.1 1.8 collective-permute-start.7
  142.9 4.0 %fusion.9 = (f32[32,4,4096]{2,1,0:T(4,128)S(1)}, f32[32,4,4096]{2,1,0:T(4,128)}) fusion(f32[64,4,4096]{2,1,0:T(4,128)} %bitcast.39), kind=kLoop, calls=%fused_computation.30 | loop fusion | bytes 8388608 | tf_op jit(solution)/shard_map/triangular_solve | solution.py:40
  146.9 1.7 triangular_solve.66
  148.6 2.0 triangular_solve.71
  150.6 0.0 collective-permute-done.7
  150.7 0.1 copy.9
  150.9 11.7 %cholesky.50 = f32[128,128]{1,0:T(8,128)S(1)} custom-call(f32[128,128]{1,0:T(8,128)S(1)} %cholesky.118), custom_call_target="Cholesky" | custom-call | tf_op jit(solution)/shard_map/jit(cholesky)/cholesky | solution.py:37
  162.6 9.8 %custom-call.14 = f32[1,128,128]{1,2,0:T(8,128)S(1)} custom-call(f32[1,128,128]{2,1,0:T(8,128)S(1)} %get-tuple-element.27), custom_call_target="InvertDiagBlocksLowerTriangular" | custom-call | tf_op jit(solution)/shard_map/jit(cholesky)/cholesky | solution.py:37
  172.5 0.2 constant_dynamic-update-slice_fusion
  172.7 0.3 slice_subtract_fusion
  172.9 11.7 %cholesky.105 = f32[128,128]{1,0:T(8,128)S(1)} custom-call(f32[128,128]{1,0:T(8,128)S(1)} %slice_subtract_fusion), custom_call_target="Cholesky" | custom-call | tf_op jit(solution)/shard_map/jit(cholesky)/cholesky | solution.py:37
  184.7 0.7 compare_reduce_fusion
  186.7 0.1 triangular_solve.61
  186.7 3.9 %while.1 = (s32[]{:T(128)}, f32[256,256]{1,0:T(8,128)S(1)}, s32[2,2]{1,0:T(2,128)S(1)}, f32[2,128,128]{2,1,0:T(8,128)S(1)}, s32[]{:T(128)}) while((s32[]{:T(128)}, f32[256,256]{1,0:T(8,128)S(1)}, s32[2,2]{1,0:T(2,128)S(1)}, f32[2,128,128]{2,1,0:T(8,128)S(1)}, s32[]{:T(128)}) %tuple.29), condition=%wide.while_cond, body=%wide.while_body.sunk | while | flops 2 | bytes 131189 | solution.py:40
  186.7 0.6 fusion.19
  187.3 1.4 bitcast_dynamic-update-slice_fusion.2
  188.7 0.6 fusion.19
  189.3 1.4 bitcast_dynamic-update-slice_fusion.2
  190.7 19.9 %custom-call.15 = f32[2,128,128]{1,2,0:T(8,128)S(1)} custom-call(f32[2,128,128]{2,1,0:T(8,128)S(1)} %get-tuple-element.9), custom_call_target="InvertDiagBlocksLowerTriangular" | custom-call | tf_op jit(solution)/shard_map/triangular_solve | solution.py:40
  210.6 3.5 %fusion.4 = f32[128,4096]{1,0:T(8,128)S(1)} fusion(f32[128,4096]{1,0:T(8,128)} %triangular_solve.66, f32[2,128,128]{1,2,0:T(8,128)S(1)} %custom-call.15), kind=kOutput, calls=%fused_computation.13 | convolution fusion | flops 805306368 | bytes 4259840 | tf_op jit(solution)/shard_map/triangular_solve | solution.py:40
  214.1 2.0 convolution_subtract_fusion
  216.1 1.9 fusion.3
  218.0 2.6 %maximum_multiply_fusion = f32[256,4096]{1,0:T(8,128)} fusion(f32[128,4096]{1,0:T(8,128)S(1)} %fusion.3, f32[128,4096]{1,0:T(8,128)S(1)} %fusion.4), kind=kLoop, calls=%fused_computation.3 | loop fusion | flops 2097152 | bytes 8388608 | tf_op jit(solution)/shard_map/mul | solution.py:44
  220.6 0.6 multiply_bitcast_fusion
  (18 shorter events, 0.5 us)
Async XLA Ops:
  80.3 14.0 %collective-permute-start = (f32[256,256]{0,1:T(8,128)S(1)}, f32[256,256]{0,1:T(8,128)S(1)}, u32[]{:S(2)}, u32[]{:S(2)}) collective-permute-start(f32[256,256]{0,1:T(8,128)S(1)} %fusion.10), channel_id=1, source_target_pairs={{0,64},{64,0},{128,192},{192,128},{1,65},{65,1},{129,193},{193,129... | collective-permute-start | bytes 786440 | tf_op jit(solution)/shard_map/ppermute | solution.py:8
  94.3 17.0 %collective-permute-start.1 = (f32[256,256]{0,1:T(8,128)S(1)}, f32[256,256]{0,1:T(8,128)S(1)}, u32[]{:S(2)}, u32[]{:S(2)}) collective-permute-start(f32[256,256]{0,1:T(8,128)S(1)} %add.49), channel_id=1, source_target_pairs={{0,128},{64,192},{128,0},{192,64},{1,129},{65,193},{129,1},{193,65... | collective-permute-start | bytes 786440 | tf_op jit(solution)/shard_map/ppermute | solution.py:8
  111.4 2.6 %collective-permute-start.2 = (f32[256,256]{0,1:T(8,128)S(1)}, f32[256,256]{0,1:T(8,128)S(1)}, u32[]{:S(2)}, u32[]{:S(2)}) collective-permute-start(f32[256,256]{0,1:T(8,128)S(1)} %add.50), channel_id=1, source_target_pairs={{0,1},{1,0},{2,3},{3,2},{4,5},{5,4},{6,7},{7,6},{8,9},{9,8},{10,11... | collective-permute-start | bytes 786440 | tf_op jit(solution)/shard_map/ppermute | solution.py:8
  114.0 7.6 %collective-permute-start.3 = (f32[256,256]{0,1:T(8,128)S(1)}, f32[256,256]{0,1:T(8,128)S(1)}, u32[]{:S(2)}, u32[]{:S(2)}) collective-permute-start(f32[256,256]{0,1:T(8,128)S(1)} %add.51), channel_id=1, source_target_pairs={{0,2},{1,3},{2,0},{3,1},{4,6},{5,7},{6,4},{7,5},{8,10},{9,11},{10,... | collective-permute-start | bytes 786440 | tf_op jit(solution)/shard_map/ppermute | solution.py:8
  121.7 6.7 %collective-permute-start.4 = (f32[256,256]{0,1:T(8,128)S(1)}, f32[256,256]{0,1:T(8,128)S(1)}, u32[]{:S(2)}, u32[]{:S(2)}) collective-permute-start(f32[256,256]{0,1:T(8,128)S(1)} %add.52), channel_id=1, source_target_pairs={{0,4},{1,5},{2,6},{3,7},{4,0},{5,1},{6,2},{7,3},{8,12},{9,13},{10,... | collective-permute-start | bytes 786440 | tf_op jit(solution)/shard_map/ppermute | solution.py:8
  128.4 7.3 %collective-permute-start.5 = (f32[256,256]{0,1:T(8,128)S(1)}, f32[256,256]{0,1:T(8,128)S(1)}, u32[]{:S(2)}, u32[]{:S(2)}) collective-permute-start(f32[256,256]{0,1:T(8,128)S(1)} %add.53), channel_id=1, source_target_pairs={{0,8},{1,9},{2,10},{3,11},{4,12},{5,13},{6,14},{7,15},{8,0},{9,1},... | collective-permute-start | bytes 786440 | tf_op jit(solution)/shard_map/ppermute | solution.py:8
  135.7 5.3 %collective-permute-start.6 = (f32[256,256]{0,1:T(8,128)S(1)}, f32[256,256]{0,1:T(8,128)S(1)}, u32[]{:S(2)}, u32[]{:S(2)}) collective-permute-start(f32[256,256]{0,1:T(8,128)S(1)} %add.54), channel_id=1, source_target_pairs={{0,16},{1,17},{2,18},{3,19},{4,20},{5,21},{6,22},{7,23},{8,24},{9,... | collective-permute-start | bytes 786440 | tf_op jit(solution)/shard_map/ppermute | solution.py:8
  141.1 9.6 %collective-permute-start.7 = (f32[256,256]{0,1:T(8,128)S(1)}, f32[256,256]{0,1:T(8,128)S(1)}, u32[]{:S(2)}, u32[]{:S(2)}) collective-permute-start(f32[256,256]{0,1:T(8,128)S(1)} %add.55), channel_id=1, source_target_pairs={{0,32},{1,33},{2,34},{3,35},{4,36},{5,37},{6,38},{7,39},{8,40},{9,... | collective-permute-start | bytes 786440 | tf_op jit(solution)/shard_map/ppermute | solution.py:8
where the time goes:
time: 225 us; the launch traced here: 221 us
  blocking collectives  62.5 us (28%)
  other arithmetic  57.4 us (26%)
  waiting for transfers between devices  48.1 us (21%)
  matrix products  19.8 us (9%)
  local copies, waits for them, and re-layouts  17.2 us (8%)
  starting transfers between devices  14.2 us (6%)
    all_to_all x1, blocking collectives, body(): lax.all_to_all(snapshots, 'wr', split_axis=1, concat_axis=0, tiled=True)  62.5 us
    ppermute x8, waiting for transfers between devices, partner(): lax.ppermute(value, axis, [(i, i ^ 1 << stride) for i in range(lax.axis_s...  48.1 us
    another operation x6, other arithmetic, body(): lower = jnp.linalg.cholesky(total)  34 us
    another operation x3, other arithmetic, body(): lax.linalg.triangular_solve(lower, regrouped, left_side=True, lower=True)  19.9 us
    ppermute x8, starting transfers between devices, partner(): lax.ppermute(value, axis, [(i, i ^ 1 << stride) for i in range(lax.axis_s...  14.2 us
    dot_general x1, matrix products, products(): lax.dot_general(left, right, (((1,), (1,)), ((), ())), precision=lax.Prec...  11.9 us
    another operation x4, local copies, waits for them, and re-layouts, body(): lax.linalg.triangular_solve(lower, regrouped, left_side=True, lower=True)  7.82 us
    another operation x3, matrix products, body(): lax.linalg.triangular_solve(lower, regrouped, left_side=True, lower=True)  7.4 us
  transfers between devices with their start and end apart: 8, of which 7 were waited for; matrix products, arithmetic and copies ran while one was open for 4% of the time, Pallas kernels for 0%

commit v1 on v0

v1 whole, which is shorter than its diff:
```python
import functools

import jax
import jax.numpy as jnp
from jax import lax
from jax.experimental import pallas as pl
from jax.experimental.pallas import tpu as pltpu
from jax.sharding import PartitionSpec as P

F32 = jnp.float32
BF = jnp.bfloat16
MESH = pl.DeviceIdType.MESH

def split3(v):
    hi=v.astype(BF); r=v-hi.astype(F32); mid=r.astype(BF); lo=(r-mid.astype(F32)).astype(BF)
    return hi,mid,lo

def rsqrt_exact(d):
    y=lax.rsqrt(d)
    return y*(1.5-0.5*d*y*y)

def factor(a_ref, v_ref, u_ref, b):
    n=a_ref.shape[0]; halves=n//128; groups=b//8
    lane=lax.broadcasted_iota(jnp.int32,(8,128),1); row=lax.broadcasted_iota(jnp.int32,(8,128),0)
    lane_all=lax.broadcasted_iota(jnp.int32,(n,n),1)
    lane_b=lax.broadcasted_iota(jnp.int32,(b,n),1); row_b=lax.broadcasted_iota(jnp.int32,(b,n),0)
    def panel(p,carry):
        k=pl.multiple_of(p*b,b)
        P=pltpu.roll(a_ref[pl.ds(k,b),:],lax.rem(n-k,n),1)
        G=[[P[8*g:8*g+8,128*h:128*h+128] for h in range(halves)] for g in range(groups)]
        UD=[None]*groups
        for q in range(groups):
            W=[{g:jnp.broadcast_to(G[g][0][:,8*q+j:8*q+j+1],(8,128)) for g in range(q,groups)} for j in range(8)]
            own=(lane>=8*q)&(lane<8*q+8)
            for g in range(q,groups):
                G[g][0]=jnp.where(own,(jnp.where(lane==row+8*q,1.0,0.0) if g==q else 0.0),G[g][0])
            dv=jnp.ones((8,128),F32)
            for j in range(8):
                d=W[j][q][j:j+1,:]
                r=1.0/d
                dv=jnp.where(row==j,d,dv)
                m={g:W[j][g]*r for g in range(q,groups)}
                m[q]=jnp.where(row>j,m[q],0.0)
                for jj in range(j+1,8):
                    pv=W[jj][q][j:j+1,:]
                    for g in range(q,groups): W[jj][g]=W[jj][g]-m[g]*pv
                pr=[G[q][h][j:j+1,:] for h in range(halves)]
                for g in range(q,groups):
                    for h in range(halves): G[g][h]=G[g][h]-m[g]*pr[h]
            s=rsqrt_exact(dv)
            ud=jnp.zeros((8,128),F32)
            for j in range(8): ud=jnp.where((lane==8*q+j)&(row<=j),W[j][q],ud)
            UD[q]=ud*s
            for h in range(halves): G[q][h]=G[q][h]*s
        Pf=jnp.concatenate([jnp.concatenate(g,axis=1) for g in G],axis=0)
        Pn=pltpu.roll(Pf,k,1)
        h3,m3,l3=split3(jnp.where((lane_b>row_b+k)&(lane_b<k+b),0.0,Pn))
        A=jnp.concatenate([h3,h3,m3,h3,l3,m3],axis=0)
        B=jnp.concatenate([h3,m3,h3,l3,h3,m3],axis=0)
        upd=lax.dot_general(A,B,(((0,),(0,)),((),())),preferred_element_type=F32)
        inpan=(lane_all>=k)&(lane_all<k+b)
        a_ref[...]=jnp.where(inpan,0.0,a_ref[...])-upd
        blk=(row_b//8)*8
        v_ref[pl.ds(k,b),:]=jnp.where(lane_b<=row_b+k,Pn,0.0)
        UDp=jnp.concatenate([jnp.concatenate([UD[g]]+[jnp.zeros((8,128),F32)]*(halves-1),axis=1) for g in range(groups)],axis=0)
        UDn=pltpu.roll(UDp,k,1)
        u_ref[pl.ds(k,b),:]=jnp.where(lane_b>=blk+k+8,Pn,UDn)
        return carry
    lax.fori_loop(0,n//b,panel,0)

def finish_kernel(b,cw,nz,g_ref,x_hbm,o_hbm,r_ref,a,v,u,xb,ob,xs,os):
    n,cells=x_hbm.shape; nch=cells//cw
    w=lax.axis_index("wr")
    loads=[pltpu.make_async_copy(x_hbm.at[:,pl.ds(i*cw,cw)],xb.at[:,pl.ds(i*cw,cw)],xs.at[i]) for i in range(nch)]
    for c in loads: c.start()
    a[...]=g_ref[...]
    factor(a,v,u,b)
    vh,vm,vl=split3(v[...]*1024.0)
    outs=[]
    for i in range(nch):
        loads[i].wait()
        xh,xm,xl=split3(xb[:,i*cw:(i+1)*cw])
        f=lambda p,q: jnp.dot(p,q,preferred_element_type=F32)
        acc=(f(vl,xh)+f(vh,xl)+f(vm,xm))+(f(vh,xm)+f(vm,xh))+f(vh,xh)
        ob[:,i*cw:(i+1)*cw]=acc
        c=pltpu.make_async_copy(ob.at[:,pl.ds(i*cw,cw)],o_hbm.at[:,pl.ds(i*cw,cw)],os.at[i]); c.start(); outs.append(c)
    ur=pltpu.roll(u[...],lax.rem(256-4*w,256),1)
    r_ref[...]=ur[:,0:4]*(1.0/1024.0)
    for c in outs: c.wait()

def finish(gram,x,b=64,cw=512):
    n,cells=x.shape
    return pl.pallas_call(functools.partial(finish_kernel,b,cw,0),
        out_shape=(jax.ShapeDtypeStruct((n,cells),F32),jax.ShapeDtypeStruct((n,4),F32)),
        in_specs=[pl.BlockSpec(memory_space=pltpu.VMEM),pl.BlockSpec(memory_space=pl.ANY)],
        out_specs=(pl.BlockSpec(memory_space=pl.ANY),pl.BlockSpec(memory_space=pltpu.VMEM)),
        scratch_shapes=[pltpu.VMEM((n,n),F32)]*3+[pltpu.VMEM((n,cells),F32)]*2+[pltpu.SemaphoreType.DMA((cells//cw,))]*2,
        compiler_params=pltpu.CompilerParams(vmem_limit_bytes=40<<20))(gram,x)


def to_peer(src, dst, send_sem, recv_sem, g, w):
    return pltpu.make_async_remote_copy(
        src_ref=src, dst_ref=dst, send_sem=send_sem, recv_sem=recv_sem, device_id=(g, w), device_id_type=MESH
    )


def wait_bytes(ref, sem):
    pltpu.make_async_copy(ref, ref, sem).wait()


def regroup_kernel(chunks, x_hbm, cells_hbm, gram_ref, buf, local, pieces, groups, total, send, recv, small, save):
    g, w = lax.axis_index("grp"), lax.axis_index("wr")
    snaps, own = buf.shape
    width = own // chunks
    rows = x_hbm.shape[0]
    writers = snaps // rows

    barrier = pltpu.get_barrier_semaphore()

    def greet(o, carry):
        pl.semaphore_signal(barrier, inc=1, device_id=(g, w ^ o), device_id_type=MESH)
        return carry

    lax.fori_loop(1, writers, greet, 0)
    for o in range(1, 4):
        pl.semaphore_signal(barrier, inc=1, device_id=(g ^ o, w), device_id_type=MESH)
    pl.semaphore_wait(barrier, writers - 1 + 3)

    mine = pl.ds(pl.multiple_of(w * rows, rows), rows)
    for c in range(chunks):

        def send_one(i, carry, c=c):
            p = w ^ lax.rem(i * 37 + w * 13 + c * 11, writers)
            src = x_hbm.at[:, pl.ds(pl.multiple_of(p * own + c * width, 128), width)]
            dst = buf.at[mine, pl.ds(c * width, width)]

            @pl.when(p == w)
            def _():
                pltpu.make_async_copy(src, dst, recv.at[c]).start()

            @pl.when(p != w)
            def _():
                to_peer(src, dst, send.at[0], recv.at[c], g, p).start()

            return carry

        lax.fori_loop(0, writers, send_one, 0)

    for c in range(chunks):
        part = buf.at[:, pl.ds(c * width, width)]
        wait_bytes(part, recv.at[c])
        pltpu.make_async_copy(part, cells_hbm.at[:, pl.ds(c * width, width)], save.at[c]).start()
        hi, mid, lo = split3(part[...])
        dot = lambda p, q: lax.dot_general(p, q, (((1,), (1,)), ((), ())), preferred_element_type=F32)
        cross = dot(hi, mid) + dot(hi, lo)
        term = (cross + cross.T) + dot(mid, mid) + dot(hi, hi)
        if c == 0:
            local[...] = term
        else:
            local[...] += term

    def scatter(o, carry):
        p = w ^ o
        to_peer(local.at[pl.ds(pl.multiple_of(p * rows, rows), rows), :], pieces.at[w], send.at[1], small.at[0], g, p).start()
        return carry

    pltpu.make_async_copy(local.at[mine, :], pieces.at[w], small.at[0]).start()
    lax.fori_loop(1, writers, scatter, 0)
    wait_bytes(pieces, small.at[0])
    groups[g] = jnp.sum(pieces[...], axis=0)
    for o in range(1, 4):
        to_peer(groups.at[g], groups.at[g], send.at[2], small.at[1], g ^ o, w).start()
    wait_bytes(groups.at[pl.ds(0, 3)], small.at[1])
    total[...] = (groups[0] + groups[1]) + (groups[2] + groups[3])

    def spread(o, carry):
        to_peer(total, gram_ref.at[mine, :], send.at[3], small.at[2], g, w ^ o).start()
        return carry

    pltpu.make_async_copy(total, gram_ref.at[mine, :], small.at[2]).start()
    lax.fori_loop(1, writers, spread, 0)
    wait_bytes(gram_ref, small.at[2])
    wait_bytes(x_hbm.at[:, pl.ds(0, (writers - 1) * own)], send.at[0])
    wait_bytes(pieces.at[pl.ds(0, writers - 1)], send.at[1])
    wait_bytes(groups.at[pl.ds(0, 3)], send.at[2])
    wait_bytes(pieces.at[pl.ds(0, writers - 1)], send.at[3])
    for c in range(chunks):
        wait_bytes(buf.at[:, pl.ds(c * width, width)], save.at[c])


def regroup(x, chunks=4):
    rows, cells = x.shape
    writers = lax.axis_size("wr")
    snaps, own = rows * writers, cells // writers
    return pl.pallas_call(
        functools.partial(regroup_kernel, chunks),
        out_shape=(jax.ShapeDtypeStruct((snaps, own), F32), jax.ShapeDtypeStruct((snaps, snaps), F32)),
        in_specs=[pl.BlockSpec(memory_space=pl.ANY)],
        out_specs=(pl.BlockSpec(memory_space=pl.ANY), pl.BlockSpec(memory_space=pltpu.VMEM)),
        scratch_shapes=[
            pltpu.VMEM((snaps, own), F32),
            pltpu.VMEM((snaps, snaps), F32),
            pltpu.VMEM((writers, rows, snaps), F32),
            pltpu.VMEM((4, rows, snaps), F32),
            pltpu.VMEM((rows, snaps), F32),
            pltpu.SemaphoreType.DMA((4,)),
            pltpu.SemaphoreType.DMA((chunks,)),
            pltpu.SemaphoreType.DMA((3,)),
            pltpu.SemaphoreType.DMA((chunks,)),
        ],
        compiler_params=pltpu.CompilerParams(
            collective_id=0, has_side_effects=True, vmem_limit_bytes=40 << 20
        ),
    )(x)


def body(snapshots):
    cells, gram = regroup(snapshots)
    return finish(gram, cells)


def solution(mesh):
    return jax.shard_map(
        body,
        mesh=mesh,
        in_specs=(P("wr", "grp"),),
        out_specs=(P(None, ("grp", "wr")), P(None, "wr")),
        check_vma=False,
    )
```

time: 225 us -> 97.2 us (0.43); the launches traced: 221 us -> 97.1 us
  Pallas kernels: 0 us -> 93.6 us
  blocking collectives: 62.5 us -> 0 us
  other arithmetic: 57.4 us -> 0 us
  waiting for transfers between devices: 48.1 us -> 0 us
  matrix products: 19.8 us -> 0 us
  local copies, waits for them, and re-layouts: 17.2 us -> 2.85 us
  starting transfers between devices: 14.2 us -> 0 us
    pallas_call x0 -> x2, Pallas kernels: none -> 93.6 us  [the longest x1 78.5 us: regroup(): pl.pallas_call(functools.partial(regroup_kernel, chunks), out_shape=(jax....]
    all_to_all x1 -> x0, blocking collectives: 62.5 us -> none  [body(): lax.all_to_all(snapshots, 'wr', split_axis=1, concat_axis=0, tiled=True)]
    another operation x9 -> x0, other arithmetic: 53.9 us -> none  [the longest x6 34 us: body(): lower = jnp.linalg.cholesky(total)]
    ppermute x8 -> x0, waiting for transfers between devices: 48.1 us -> none  [partner(): lax.ppermute(value, axis, [(i, i ^ 1 << stride) for i in range(lax.axis_s...]
    ppermute x8 -> x0, starting transfers between devices: 14.2 us -> none  [partner(): lax.ppermute(value, axis, [(i, i ^ 1 << stride) for i in range(lax.axis_s...]
    dot_general x1 -> x0, matrix products: 11.9 us -> none  [products(): lax.dot_general(left, right, (((1,), (1,)), ((), ())), precision=lax.Prec...]
    another operation x12 -> x0, local copies, waits for them, and re-layouts: 11.8 us -> none  [the longest x4 7.82 us: body(): lax.linalg.triangular_solve(lower, regrouped, left_side=True, lower=True)]
    another operation x5 -> x0, matrix products: 7.87 us -> none  [the longest x3 7.4 us: body(): lax.linalg.triangular_solve(lower, regrouped, left_side=True, lower=True)]
  transfers between devices with their start and end apart: 8 -> 0, of which waited for: 7 -> 0; matrix products, arithmetic and copies ran while one was open for 4% -> 0% of each run, Pallas kernels for 0% -> 0%
where the time goes in v1:
time: 97.2 us; the launch traced here: 97.1 us
  Pallas kernels  93.6 us (96%)
  local copies, waits for them, and re-layouts  2.85 us (3%)
    pallas_call x1, Pallas kernels, regroup(): pl.pallas_call(functools.partial(regroup_kernel, chunks), out_shape=(jax....  78.5 us
    pallas_call x1, Pallas kernels, finish(): pl.pallas_call(functools.partial(finish_kernel, b, cw, 0), out_shape=(jax...  15 us
    unnamed x2, local copies, waits for them, and re-layouts  2.18 us

profile of v1, /device:TPU:1, one launch (start us, length us, event | category | flops | bytes accessed | tf_op | source)
XLA Modules:
  0.0 97.1 jit_solution(8770244872240068822)
XLA Ops:
  0.6 0.0 copy-start
  0.6 2.2 %copy-done = f32[4,262144]{1,0:T(4,128)S(1)} copy-done((f32[4,262144]{1,0:T(4,128)S(1)}, f32[4,262144]{1,0:T(4,128)}, u32[]{:S(2)}) %copy-start) | copy-done | bytes 4194328
  2.8 78.5 %shard_map.30 = (f32[256,4096]{1,0:T(8,128)S(1)}, f32[256,256]{1,0:T(8,128)S(1)}) custom-call(f32[4,262144]{1,0:T(4,128)S(1)} %copy-done), custom_call_target="tpu_custom_call" | custom-call | tf_op jit(solution)/shard_map/pallas_call | solution.py:195
  81.4 15.0 %shard_map.31 = (f32[256,4096]{1,0:T(8,128)}, f32[256,4]{1,0:T(8,128)S(1)}) custom-call(f32[256,256]{1,0:T(8,128)S(1)} %get-tuple-element.4.g_ref, f32[256,4096]{1,0:T(8,128)S(1)} %get-tuple-element.5.x_hbm), custom_call_target="tpu_custom_call" | custom-call | tf_op jit(solution)/shard_map/pallas_call | solution.py:93
  96.4 0.7 copy.3
Async XLA Ops:
  0.6 2.2 %copy-start = (f32[4,262144]{1,0:T(4,128)S(1)}, f32[4,262144]{1,0:T(4,128)}, u32[]{:S(2)}) copy-start(f32[4,262144]{1,0:T(4,128)} %x_hbm.1) | copy-start | bytes 12582916

commit v2 on v1

v2 whole, which is shorter than its diff:
```python
import functools

import jax
import jax.numpy as jnp
from jax import lax
from jax.experimental import pallas as pl
from jax.experimental.pallas import tpu as pltpu
from jax.sharding import PartitionSpec as P

F32 = jnp.float32
BF = jnp.bfloat16
MESH = pl.DeviceIdType.MESH

CHUNKS = ((0, 3072), (3072, 1024))

def split3(v):
    hi=v.astype(BF); r=v-hi.astype(F32); mid=r.astype(BF); lo=(r-mid.astype(F32)).astype(BF)
    return hi,mid,lo

def rsqrt_exact(d):
    y=lax.rsqrt(d)
    return y*(1.5-0.5*d*y*y)

def factor(a_ref, v_ref, u_ref, b):
    n=a_ref.shape[0]; halves=n//128; groups=b//8
    lane=lax.broadcasted_iota(jnp.int32,(8,128),1); row=lax.broadcasted_iota(jnp.int32,(8,128),0)
    lane_all=lax.broadcasted_iota(jnp.int32,(n,n),1)
    lane_b=lax.broadcasted_iota(jnp.int32,(b,n),1); row_b=lax.broadcasted_iota(jnp.int32,(b,n),0)
    def panel(p,carry):
        k=pl.multiple_of(p*b,b)
        P=pltpu.roll(a_ref[pl.ds(k,b),:],lax.rem(n-k,n),1)
        G=[[P[8*g:8*g+8,128*h:128*h+128] for h in range(halves)] for g in range(groups)]
        UD=[None]*groups
        for q in range(groups):
            W=[{g:jnp.broadcast_to(G[g][0][:,8*q+j:8*q+j+1],(8,128)) for g in range(q,groups)} for j in range(8)]
            own=(lane>=8*q)&(lane<8*q+8)
            for g in range(q,groups):
                G[g][0]=jnp.where(own,(jnp.where(lane==row+8*q,1.0,0.0) if g==q else 0.0),G[g][0])
            dv=jnp.ones((8,128),F32)
            for j in range(8):
                d=W[j][q][j:j+1,:]
                r=1.0/d
                dv=jnp.where(row==j,d,dv)
                m={g:W[j][g]*r for g in range(q,groups)}
                m[q]=jnp.where(row>j,m[q],0.0)
                for jj in range(j+1,8):
                    pv=W[jj][q][j:j+1,:]
                    for g in range(q,groups): W[jj][g]=W[jj][g]-m[g]*pv
                pr=[G[q][h][j:j+1,:] for h in range(halves)]
                for g in range(q,groups):
                    for h in range(halves): G[g][h]=G[g][h]-m[g]*pr[h]
            s=rsqrt_exact(dv)
            ud=jnp.zeros((8,128),F32)
            for j in range(8): ud=jnp.where((lane==8*q+j)&(row<=j),W[j][q],ud)
            UD[q]=ud*s
            for h in range(halves): G[q][h]=G[q][h]*s
        Pf=jnp.concatenate([jnp.concatenate(g,axis=1) for g in G],axis=0)
        Pn=pltpu.roll(Pf,k,1)
        h3,m3,l3=split3(jnp.where((lane_b>row_b+k)&(lane_b<k+b),0.0,Pn))
        A=jnp.concatenate([h3,h3,m3,h3,l3,m3],axis=0)
        B=jnp.concatenate([h3,m3,h3,l3,h3,m3],axis=0)
        upd=lax.dot_general(A,B,(((0,),(0,)),((),())),preferred_element_type=F32)
        inpan=(lane_all>=k)&(lane_all<k+b)
        a_ref[...]=jnp.where(inpan,0.0,a_ref[...])-upd
        blk=(row_b//8)*8
        v_ref[pl.ds(k,b),:]=jnp.where(lane_b<=row_b+k,Pn,0.0)
        UDp=jnp.concatenate([jnp.concatenate([UD[g]]+[jnp.zeros((8,128),F32)]*(halves-1),axis=1) for g in range(groups)],axis=0)
        UDn=pltpu.roll(UDp,k,1)
        u_ref[pl.ds(k,b),:]=jnp.where(lane_b>=blk+k+8,Pn,UDn)
        return carry
    lax.fori_loop(0,n//b,panel,0)

def finish_kernel(b, cw, g_ref, x_ref, o_hbm, r_ref, a, v, u, ob, out_sem):
    n, cells = x_ref.shape
    w = lax.axis_index("wr")
    a[...] = g_ref[...]
    factor(a, v, u, b)
    vh, vm, vl = split3(v[...] * 1024.0)
    outs = []
    for i in range(cells // cw):
        xh, xm, xl = split3(x_ref[:, i * cw : (i + 1) * cw])
        f = lambda p, q: jnp.dot(p, q, preferred_element_type=F32)
        acc = (f(vl, xh) + f(vh, xl) + f(vm, xm)) + (f(vh, xm) + f(vm, xh)) + f(vh, xh)
        ob[:, i * cw : (i + 1) * cw] = acc
        c = pltpu.make_async_copy(ob.at[:, pl.ds(i * cw, cw)], o_hbm.at[:, pl.ds(i * cw, cw)], out_sem.at[i])
        c.start()
        outs.append(c)
    turned = pltpu.roll(u[...], lax.rem(n - 4 * w, n), 1)
    r_ref[...] = turned[:, 0:128].T[0:4, :] * (1.0 / 1024.0)
    for c in outs:
        c.wait()


def finish(gram, x, b=64, cw=512):
    n, cells = x.shape
    return pl.pallas_call(
        functools.partial(finish_kernel, b, cw),
        out_shape=(jax.ShapeDtypeStruct((n, cells), F32), jax.ShapeDtypeStruct((4, n), F32)),
        in_specs=[pl.BlockSpec(memory_space=pltpu.VMEM), pl.BlockSpec(memory_space=pltpu.VMEM)],
        out_specs=(pl.BlockSpec(memory_space=pltpu.HBM), pl.BlockSpec(memory_space=pltpu.VMEM)),
        scratch_shapes=[pltpu.VMEM((n, n), F32)] * 3 + [pltpu.VMEM((n, cells), F32), pltpu.SemaphoreType.DMA((cells // cw,))],
        compiler_params=pltpu.CompilerParams(vmem_limit_bytes=40 << 20),
    )(gram, x)


def to_peer(src, dst, send_sem, recv_sem, peer):
    return pltpu.make_async_remote_copy(
        src_ref=src, dst_ref=dst, send_sem=send_sem, recv_sem=recv_sem, device_id=peer, device_id_type=MESH
    )


def wait_bytes(ref, sem):
    pltpu.make_async_copy(ref, ref, sem).wait()


ORDER = (
    (0, 3, 1, 1),
    (2, 1, 1, 0),
    (3, 3, 0, 0),
    (0, 1, 1, 0),
    (2, 3, 0, 0),
    (0, 2, 0, 0),
    (1, 0, 1, 1),
    (3, 1, 0, 0),
    (2, 2, 1, 0),
    (1, 0, 1, 0),
    (3, 2, 0, 0),
    (2, 2, 1, 1),
    (2, 3, 1, 0),
    (0, 1, 0, 0),
    (0, 0, 0, 1),
    (2, 3, 0, 1),
    (3, 3, 1, 0),
    (1, 1, 1, 1),
    (1, 2, 0, 0),
    (3, 0, 1, 1),
    (2, 2, 0, 0),
    (0, 1, 0, 1),
    (0, 3, 1, 0),
    (2, 0, 0, 0),
    (0, 0, 1, 0),
    (2, 1, 0, 1),
    (0, 3, 0, 0),
    (0, 1, 1, 1),
    (3, 3, 0, 1),
    (2, 0, 1, 1),
    (1, 2, 0, 1),
    (3, 2, 1, 0),
    (1, 1, 1, 0),
    (2, 3, 1, 1),
    (0, 2, 0, 1),
    (3, 0, 0, 1),
    (1, 3, 0, 0),
    (3, 1, 1, 0),
    (1, 0, 0, 0),
    (3, 1, 0, 1),
    (1, 3, 1, 0),
    (3, 2, 0, 1),
    (1, 2, 1, 1),
    (0, 0, 1, 1),
    (3, 0, 0, 0),
    (1, 3, 0, 1),
    (2, 1, 1, 1),
    (0, 2, 1, 1),
    (2, 1, 0, 0),
    (0, 3, 0, 1),
    (3, 0, 1, 0),
    (1, 3, 1, 1),
    (1, 1, 0, 0),
    (1, 2, 1, 0),
    (2, 2, 0, 1),
    (3, 3, 1, 1),
    (3, 1, 1, 1),
    (2, 0, 0, 1),
    (0, 2, 1, 0),
    (1, 0, 0, 1),
    (3, 2, 1, 1),
    (1, 1, 0, 1),
    (2, 0, 1, 0),
)
RING = tuple(range(1, 8))


def regroup_kernel(chunks, x_hbm, cells_ref, gram_ref, staged, local, other, half, pieces, layers, total, send, recv, small, load):
    g, w = lax.axis_index("grp"), lax.axis_index("wr")
    snaps, own = cells_ref.shape
    rows = x_hbm.shape[0]
    writers = snaps // rows
    core, zlo, place = lax.rem(w, 2), lax.rem(w // 2, 2), w // 4
    x, y = lax.rem(place, 4), place // 4

    pieces_in = 4
    span = x_hbm.shape[1] // pieces_in
    loads = [
        pltpu.make_async_copy(x_hbm.at[:, pl.ds(i * span, span)], staged.at[:, pl.ds(i * span, span)], load.at[i])
        for i in range(pieces_in)
    ]
    for copy in loads:
        copy.start()

    def peer(offset):
        dy, dx, dz, dc = offset
        at_y, at_x = lax.rem(y + dy, 4), lax.rem(x + dx, 4)
        return g, ((at_y * 4 + at_x) * 2 + lax.rem(zlo + dz, 2)) * 2 + lax.rem(core + dc, 2)

    def along_z(step):
        z = lax.rem(g * 2 + zlo + step, 8)
        return z // 2, w + 2 * (lax.rem(z, 2) - zlo)

    barrier = pltpu.get_barrier_semaphore()

    def greet(to):
        pl.semaphore_signal(barrier, inc=1, device_id=to, device_id_type=MESH)

    def greet_group(o, carry):
        greet((g, w ^ o))
        return carry

    def greet_ring(step, carry):
        to = along_z(step)

        @pl.when(to[0] != g)
        def _():
            greet(to)

        return carry

    lax.fori_loop(1, 8, greet_ring, 0)
    lax.fori_loop(1, writers, greet_group, 0)
    pl.semaphore_wait(barrier, writers - 1 + 6)
    for copy in loads:
        copy.wait()

    mine = pl.ds(pl.multiple_of(w * rows, rows), rows)
    for c, (first, width) in enumerate(chunks):
        at = pl.ds(first, width)

        def source(p):
            return staged.at[:, pl.ds(pl.multiple_of(p * own + first, 128), width)]

        for o in ORDER:
            to = peer(o)
            to_peer(source(to[1]), cells_ref.at[mine, at], send.at[0], recv.at[c], to).start()
        pltpu.make_async_copy(source(w), cells_ref.at[mine, at], recv.at[c]).start()

    dot = lambda p, q: lax.dot_general(p, q, (((1,), (1,)), ((), ())), preferred_element_type=F32)
    for c, (first, width) in enumerate(chunks):
        part = cells_ref.at[:, pl.ds(first, width)]
        wait_bytes(part, recv.at[c])
        hi, mid, lo = split3(part[...])
        small_terms = (dot(hi, lo) + dot(lo, hi) + dot(mid, mid)) + (dot(hi, mid) + dot(mid, hi))
        term = small_terms + dot(hi, hi)
        local[...] = term if c == 0 else local[...] + term

    deep = snaps // 2
    strip = deep // 16
    to_peer(
        local.at[pl.ds(pl.multiple_of((1 - core) * deep, deep), deep), :], other, send.at[1], small.at[0], (g, w ^ 1)
    ).start()
    wait_bytes(other, small.at[0])
    half[...] = local[pl.ds(pl.multiple_of(core * deep, deep), deep), :] + other[...]

    def strip_of(p):
        return pl.ds(pl.multiple_of(p * strip, strip), strip)

    def scatter(o, carry):
        p = place ^ o
        to_peer(half.at[strip_of(p), :], pieces.at[place], send.at[2], small.at[1], (g, w ^ (4 * o))).start()
        return carry

    lax.fori_loop(1, 16, scatter, 0)
    pieces[place] = half[strip_of(place), :]
    wait_bytes(pieces.at[pl.ds(0, 15)], small.at[1])
    layer = g * 2 + zlo
    layers[layer] = jnp.sum(pieces[...], axis=0)
    for step in RING:
        to_peer(layers.at[layer], layers.at[layer], send.at[3], small.at[2], along_z(step)).start()
    wait_bytes(layers.at[pl.ds(0, 7)], small.at[2])
    total[...] = jnp.sum(layers[...], axis=0)
    rows_out = pl.ds(pl.multiple_of(core * deep + place * strip, strip), strip)

    def spread(o, carry):
        to_peer(total, gram_ref.at[rows_out, :], send.at[4], small.at[3], (g, w ^ (4 * (o // 2) + lax.rem(o, 2)))).start()
        return carry

    lax.fori_loop(1, 32, spread, 0)
    gram_ref[rows_out, :] = total[...]
    wait_bytes(gram_ref.at[pl.ds(0, 31 * strip), :], small.at[3])
    wait_bytes(staged.at[:, pl.ds(0, (writers - 1) * own)], send.at[0])
    wait_bytes(other, send.at[1])
    wait_bytes(pieces.at[pl.ds(0, 15)], send.at[2])
    wait_bytes(layers.at[pl.ds(0, 7)], send.at[3])
    wait_bytes(gram_ref.at[pl.ds(0, 31 * strip), :], send.at[4])


def regroup(x):
    rows, cells = x.shape
    writers = lax.axis_size("wr")
    snaps, own = rows * writers, cells // writers
    chunks = CHUNKS
    return pl.pallas_call(
        functools.partial(regroup_kernel, chunks),
        out_shape=(jax.ShapeDtypeStruct((snaps, own), F32), jax.ShapeDtypeStruct((snaps, snaps), F32)),
        in_specs=[pl.BlockSpec(memory_space=pltpu.HBM)],
        out_specs=(pl.BlockSpec(memory_space=pltpu.VMEM), pl.BlockSpec(memory_space=pltpu.VMEM)),
        scratch_shapes=[
            pltpu.VMEM((rows, cells), F32),
            pltpu.VMEM((snaps, snaps), F32),
            pltpu.VMEM((snaps // 2, snaps), F32),
            pltpu.VMEM((snaps // 2, snaps), F32),
            pltpu.VMEM((16, snaps // 32, snaps), F32),
            pltpu.VMEM((8, snaps // 32, snaps), F32),
            pltpu.VMEM((snaps // 32, snaps), F32),
            pltpu.SemaphoreType.DMA((5,)),
            pltpu.SemaphoreType.DMA((len(chunks),)),
            pltpu.SemaphoreType.DMA((4,)),
            pltpu.SemaphoreType.DMA((4,)),
        ],
        compiler_params=pltpu.CompilerParams(
            collective_id=0, has_side_effects=True, vmem_limit_bytes=48 << 20
        ),
    )(x)


def body(snapshots):
    cells, gram = regroup(snapshots)
    basis, columns = finish(gram, cells)
    return basis, columns.T


def solution(mesh):
    return jax.shard_map(
        body,
        mesh=mesh,
        in_specs=(P("wr", "grp"),),
        out_specs=(P(None, ("grp", "wr")), P(None, "wr")),
        check_vma=False,
    )
```

time: 97.2 us -> 93.4 us (0.961)
  local copies, waits for them, and re-layouts: 2.85 us -> 0 us
    unnamed x2 -> x0, local copies, waits for them, and re-layouts: 2.18 us -> none
    pallas_call x1, Pallas kernels: 15 us -> 13.5 us  [finish(): pl.pallas_call(functools.partial(finish_kernel, b, cw), out_shape=(jax.Sh...]
where the time goes in v2:
time: 93.4 us; the launch traced here: 93.3 us
  Pallas kernels  92.7 us (99%)
    pallas_call x1, Pallas kernels, regroup(): pl.pallas_call(functools.partial(regroup_kernel, chunks), out_shape=(jax....  79.2 us
    pallas_call x1, Pallas kernels, finish(): pl.pallas_call(functools.partial(finish_kernel, b, cw), out_shape=(jax.Sh...  13.5 us

profile of v2, /device:TPU:1, one launch (start us, length us, event | category | flops | bytes accessed | tf_op | source)
XLA Modules:
  0.0 93.3 jit_solution(14935579295525157474)
XLA Ops:
  0.6 79.2 %shard_map.30 = (f32[256,4096]{1,0:T(8,128)S(1)}, f32[256,256]{1,0:T(8,128)S(1)}) custom-call(f32[4,262144]{1,0:T(4,128)} %x_hbm.1), custom_call_target="tpu_custom_call" | custom-call | tf_op jit(solution)/shard_map/pallas_call | solution.py:301
  79.8 13.5 %shard_map.31 = (f32[256,4096]{1,0:T(8,128)}, f32[4,256]{1,0:T(4,128)}) custom-call(f32[256,256]{1,0:T(8,128)S(1)} %get-tuple-element.6.g_ref, f32[256,4096]{1,0:T(8,128)S(1)} %get-tuple-element.7.x_ref), custom_call_target="tpu_custom_call" | custom-call | tf_op jit(solution)/shard_map/pallas_call | solution.py:96

commit v3 on v2

--- a/solution.py
+++ b/solution.py
@@ -21,18 +21,27 @@
     y=lax.rsqrt(d)
     return y*(1.5-0.5*d*y*y)
 
-def factor(a_ref, v_ref, u_ref, b):
+def pick(rows, l):
+    where = jnp.full(rows.shape, l, jnp.int32)
+    return jnp.take_along_axis(rows, where, axis=1, mode="promise_in_bounds")
+
+
+def factor(a_ref, v_ref, u_ref, b, product, rows_out):
     n=a_ref.shape[0]; halves=n//128; groups=b//8
     lane=lax.broadcasted_iota(jnp.int32,(8,128),1); row=lax.broadcasted_iota(jnp.int32,(8,128),0)
     lane_all=lax.broadcasted_iota(jnp.int32,(n,n),1)
     lane_b=lax.broadcasted_iota(jnp.int32,(b,n),1); row_b=lax.broadcasted_iota(jnp.int32,(b,n),0)
     def panel(p,carry):
         k=pl.multiple_of(p*b,b)
+        product(jnp.maximum(p-1,0))
         P=pltpu.roll(a_ref[pl.ds(k,b),:],lax.rem(n-k,n),1)
         G=[[P[8*g:8*g+8,128*h:128*h+128] for h in range(halves)] for g in range(groups)]
         UD=[None]*groups
         for q in range(groups):
-            W=[{g:jnp.broadcast_to(G[g][0][:,8*q+j:8*q+j+1],(8,128)) for g in range(q,groups)} for j in range(8)]
+            W=[{g:pick(G[g][0],8*q+j) for g in range(q+(q>0),groups)} for j in range(8)]
+            if q>0:
+                for j in range(8): W[j][q]=ahead[j]
+            if q+1<groups: ahead=[pick(G[q+1][0],8*q+8+j) for j in range(8)]
             own=(lane>=8*q)&(lane<8*q+8)
             for g in range(q,groups):
                 G[g][0]=jnp.where(own,(jnp.where(lane==row+8*q,1.0,0.0) if g==q else 0.0),G[g][0])
@@ -46,6 +55,8 @@
                 for jj in range(j+1,8):
                     pv=W[jj][q][j:j+1,:]
                     for g in range(q,groups): W[jj][g]=W[jj][g]-m[g]*pv
+                if q+1<groups:
+                    for jj in range(8): ahead[jj]=ahead[jj]-m[q+1]*W[j][q+1][jj:jj+1,:]
                 pr=[G[q][h][j:j+1,:] for h in range(halves)]
                 for g in range(q,groups):
                     for h in range(halves): G[g][h]=G[g][h]-m[g]*pr[h]
@@ -67,40 +78,50 @@
         UDp=jnp.concatenate([jnp.concatenate([UD[g]]+[jnp.zeros((8,128),F32)]*(halves-1),axis=1) for g in range(groups)],axis=0)
         UDn=pltpu.roll(UDp,k,1)
         u_ref[pl.ds(k,b),:]=jnp.where(lane_b>=blk+k+8,Pn,UDn)
+        @pl.when(p>0)
+        def _(): rows_out(p-1).start()
         return carry
     lax.fori_loop(0,n//b,panel,0)
-
-def finish_kernel(b, cw, g_ref, x_ref, o_hbm, r_ref, a, v, u, ob, out_sem):
-    n, cells = x_ref.shape
+    product(n//b-1)
+    rows_out(n//b-1).start()
+
+def finish_kernel(b, cw, g_ref, xh_ref, xm_ref, xl_ref, o_hbm, r_ref, a, v, u, ob, out_sem):
+    n, cells = xh_ref.shape
     w = lax.axis_index("wr")
     a[...] = g_ref[...]
-    factor(a, v, u, b)
-    vh, vm, vl = split3(v[...] * 1024.0)
-    outs = []
-    for i in range(cells // cw):
-        xh, xm, xl = split3(x_ref[:, i * cw : (i + 1) * cw])
-        f = lambda p, q: jnp.dot(p, q, preferred_element_type=F32)
-        acc = (f(vl, xh) + f(vh, xl) + f(vm, xm)) + (f(vh, xm) + f(vm, xh)) + f(vh, xh)
-        ob[:, i * cw : (i + 1) * cw] = acc
-        c = pltpu.make_async_copy(ob.at[:, pl.ds(i * cw, cw)], o_hbm.at[:, pl.ds(i * cw, cw)], out_sem.at[i])
-        c.start()
-        outs.append(c)
+    v[0:b, :] = jnp.zeros((b, n), F32)
+
+    def product(p):
+        at = pl.ds(pl.multiple_of(p * b, b), b)
+        vh, vm, vl = split3(v[at, :] * 1024.0)
+        three, two = jnp.concatenate([vh, vm, vl], axis=0), jnp.concatenate([vh, vm], axis=0)
+        f = lambda l, r: jnp.dot(l, r, preferred_element_type=F32)
+        for i in range(cells // cw):
+            part = slice(i * cw, (i + 1) * cw)
+            th, tm, tl = f(three, xh_ref[:, part]), f(two, xm_ref[:, part]), f(vh, xl_ref[:, part])
+            ob[at, part] = (th[2 * b :] + tm[b:] + tl) + (th[b : 2 * b] + tm[:b]) + th[:b]
+
+    def rows_out(p):
+        at = pl.ds(pl.multiple_of(p * b, b), b)
+        return pltpu.make_async_copy(ob.at[at, :], o_hbm.at[at, :], out_sem.at[p])
+
+    factor(a, v, u, b, product, rows_out)
     turned = pltpu.roll(u[...], lax.rem(n - 4 * w, n), 1)
     r_ref[...] = turned[:, 0:128].T[0:4, :] * (1.0 / 1024.0)
-    for c in outs:
-        c.wait()
+    for p in range(n // b):
+        rows_out(p).wait()
 
 
 def finish(gram, x, b=64, cw=512):
-    n, cells = x.shape
+    n, cells = x[0].shape
     return pl.pallas_call(
         functools.partial(finish_kernel, b, cw),
         out_shape=(jax.ShapeDtypeStruct((n, cells), F32), jax.ShapeDtypeStruct((4, n), F32)),
-        in_specs=[pl.BlockSpec(memory_space=pltpu.VMEM), pl.BlockSpec(memory_space=pltpu.VMEM)],
+        in_specs=[pl.BlockSpec(memory_space=pltpu.VMEM)] * 4,
         out_specs=(pl.BlockSpec(memory_space=pltpu.HBM), pl.BlockSpec(memory_space=pltpu.VMEM)),
-        scratch_shapes=[pltpu.VMEM((n, n), F32)] * 3 + [pltpu.VMEM((n, cells), F32), pltpu.SemaphoreType.DMA((cells // cw,))],
+        scratch_shapes=[pltpu.VMEM((n, n), F32)] * 3 + [pltpu.VMEM((n, cells), F32), pltpu.SemaphoreType.DMA((n // b,))],
         compiler_params=pltpu.CompilerParams(vmem_limit_bytes=40 << 20),
-    )(gram, x)
+    )(gram, *x)
 
 
 def to_peer(src, dst, send_sem, recv_sem, peer):
@@ -181,7 +202,7 @@
 RING = tuple(range(1, 8))
 
 
-def regroup_kernel(chunks, x_hbm, cells_ref, gram_ref, staged, local, other, half, pieces, layers, total, send, recv, small, load):
+def regroup_kernel(chunks, x_hbm, high_ref, mid_ref, low_ref, gram_ref, cells_ref, staged, local, other, half, pieces, layers, total, send, recv, small, load):
     g, w = lax.axis_index("grp"), lax.axis_index("wr")
     snaps, own = cells_ref.shape
     rows = x_hbm.shape[0]
@@ -248,6 +269,8 @@
         part = cells_ref.at[:, pl.ds(first, width)]
         wait_bytes(part, recv.at[c])
         hi, mid, lo = split3(part[...])
+        at = pl.ds(first, width)
+        high_ref[:, at], mid_ref[:, at], low_ref[:, at] = hi, mid, lo
         small_terms = (dot(hi, lo) + dot(lo, hi) + dot(mid, mid)) + (dot(hi, mid) + dot(mid, hi))
         term = small_terms + dot(hi, hi)
         local[...] = term if c == 0 else local[...] + term
@@ -300,10 +323,11 @@
     chunks = CHUNKS
     return pl.pallas_call(
         functools.partial(regroup_kernel, chunks),
-        out_shape=(jax.ShapeDtypeStruct((snaps, own), F32), jax.ShapeDtypeStruct((snaps, snaps), F32)),
+        out_shape=(*[jax.ShapeDtypeStruct((snaps, own), BF)] * 3, jax.ShapeDtypeStruct((snaps, snaps), F32)),
         in_specs=[pl.BlockSpec(memory_space=pltpu.HBM)],
-        out_specs=(pl.BlockSpec(memory_space=pltpu.VMEM), pl.BlockSpec(memory_space=pltpu.VMEM)),
+        out_specs=(pl.BlockSpec(memory_space=pltpu.VMEM),) * 4,
         scratch_shapes=[
+            pltpu.VMEM((snaps, own), F32),
             pltpu.VMEM((rows, cells), F32),
             pltpu.VMEM((snaps, snaps), F32),
             pltpu.VMEM((snaps // 2, snaps), F32),
@@ -317,13 +341,13 @@
             pltpu.SemaphoreType.DMA((4,)),
         ],
         compiler_params=pltpu.CompilerParams(
-            collective_id=0, has_side_effects=True, vmem_limit_bytes=48 << 20
+            collective_id=0, has_side_effects=True, vmem_limit_bytes=46 << 20
         ),
     )(x)
 
 
 def body(snapshots):
-    cells, gram = regroup(snapshots)
+    *cells, gram = regroup(snapshots)
     basis, columns = finish(gram, cells)
     return basis, columns.T
 

time: 93.4 us -> 90.6 us (0.970)
  Pallas kernels: 92.7 us -> 89.9 us
    pallas_call x1, Pallas kernels: 13.5 us -> 10.7 us  [finish(): pl.pallas_call(functools.partial(finish_kernel, b, cw), out_shape=(jax.Sh...]
where the time goes in v3:
time: 90.6 us; the launch traced here: 90.5 us
  Pallas kernels  89.9 us (99%)
    pallas_call x1, Pallas kernels, regroup(): pl.pallas_call(functools.partial(regroup_kernel, chunks), out_shape=(*[ja...  79.2 us
    pallas_call x1, Pallas kernels, finish(): pl.pallas_call(functools.partial(finish_kernel, b, cw), out_shape=(jax.Sh...  10.7 us

profile of v3, /device:TPU:1, one launch (start us, length us, event | category | flops | bytes accessed | tf_op | source)
XLA Modules:
  0.0 90.5 jit_solution(378848875820608911)
XLA Ops:
  0.6 79.2 %shard_map.30 = (bf16[256,4096]{1,0:T(8,128)(2,1)S(1)}, bf16[256,4096]{1,0:T(8,128)(2,1)S(1)}, bf16[256,4096]{1,0:T(8,128)(2,1)S(1)}, f32[256,256]{1,0:T(8,128)S(1)}) custom-call(f32[4,262144]{1,0:T(4,128)} %x_hbm.1), custom_call_target="tpu_custom_call" | custom-call | tf_op jit(solution)/shard_map/pallas_call | solution.py:324
  79.9 10.7 %shard_map.31 = (f32[256,4096]{1,0:T(8,128)}, f32[4,256]{1,0:T(4,128)}) custom-call(f32[256,256]{1,0:T(8,128)S(1)} %get-tuple-element.8.g_ref, bf16[256,4096]{1,0:T(8,128)(2,1)S(1)} %get-tuple-element.9.xh_ref, bf16[256,4096]{1,0:T(8,128)(2,1)S(1)} %get-tuple-element.10.xm_ref, bf16[256,4096]{1,0:T(8,128)(2,1)S(1)} %get-tuple-element.11.xl_ref), custom_call_target="tpu_custom_call" | custom-call | tf_op jit(solution)/shard_map/pallas_call | solution.py:117

commit v4 on v3

--- a/solution.py
+++ b/solution.py
@@ -11,7 +11,7 @@
 BF = jnp.bfloat16
 MESH = pl.DeviceIdType.MESH
 
-CHUNKS = ((0, 3072), (3072, 1024))
+CHUNKS = ((0, 2560), (2560, 1024), (3584, 512))
 
 def split3(v):
     hi=v.astype(BF); r=v-hi.astype(F32); mid=r.astype(BF); lo=(r-mid.astype(F32)).astype(BF)
@@ -199,10 +199,12 @@
     (1, 1, 0, 1),
     (2, 0, 1, 0),
 )
-RING = tuple(range(1, 8))
-
-
-def regroup_kernel(chunks, x_hbm, high_ref, mid_ref, low_ref, gram_ref, cells_ref, staged, local, other, half, pieces, layers, total, send, recv, small, load):
+RING = (4, 3, 5, 2, 6, 1, 7)
+HOPS = (0, 1, 2, 1)
+FAR_FIRST = sorted(range(1, 32), key=lambda o: -HOPS[o // 8] - HOPS[o // 2 % 4])
+
+
+def regroup_kernel(chunks, x_hbm, high_ref, mid_ref, low_ref, gram_ref, cells_ref, staged, local, pieces, layers, total, send, recv, small, load):
     g, w = lax.axis_index("grp"), lax.axis_index("wr")
     snaps, own = cells_ref.shape
     rows = x_hbm.shape[0]
@@ -277,41 +279,28 @@
 
     deep = snaps // 2
     strip = deep // 16
-    to_peer(
-        local.at[pl.ds(pl.multiple_of((1 - core) * deep, deep), deep), :], other, send.at[1], small.at[0], (g, w ^ 1)
-    ).start()
-    wait_bytes(other, small.at[0])
-    half[...] = local[pl.ds(pl.multiple_of(core * deep, deep), deep), :] + other[...]
-
-    def strip_of(p):
-        return pl.ds(pl.multiple_of(p * strip, strip), strip)
-
-    def scatter(o, carry):
-        p = place ^ o
-        to_peer(half.at[strip_of(p), :], pieces.at[place], send.at[2], small.at[1], (g, w ^ (4 * o))).start()
-        return carry
-
-    lax.fori_loop(1, 16, scatter, 0)
-    pieces[place] = half[strip_of(place), :]
-    wait_bytes(pieces.at[pl.ds(0, 15)], small.at[1])
+
+    def rows_of(p, c):
+        return pl.ds(pl.multiple_of(c * deep + p * strip, strip), strip)
+
+    for o in FAR_FIRST:
+        p, c = place ^ (o // 2), core ^ (o % 2)
+        to_peer(local.at[rows_of(p, c), :], pieces.at[place * 2 + core], send.at[2], small.at[1], (g, w ^ (4 * (o // 2) + o % 2))).start()
+    pieces[place * 2 + core] = local[rows_of(place, core), :]
+    wait_bytes(pieces.at[pl.ds(0, 31)], small.at[1])
     layer = g * 2 + zlo
     layers[layer] = jnp.sum(pieces[...], axis=0)
     for step in RING:
         to_peer(layers.at[layer], layers.at[layer], send.at[3], small.at[2], along_z(step)).start()
     wait_bytes(layers.at[pl.ds(0, 7)], small.at[2])
     total[...] = jnp.sum(layers[...], axis=0)
-    rows_out = pl.ds(pl.multiple_of(core * deep + place * strip, strip), strip)
-
-    def spread(o, carry):
-        to_peer(total, gram_ref.at[rows_out, :], send.at[4], small.at[3], (g, w ^ (4 * (o // 2) + lax.rem(o, 2)))).start()
-        return carry
-
-    lax.fori_loop(1, 32, spread, 0)
+    rows_out = rows_of(place, core)
+    for o in FAR_FIRST:
+        to_peer(total, gram_ref.at[rows_out, :], send.at[4], small.at[3], (g, w ^ (4 * (o // 2) + o % 2))).start()
     gram_ref[rows_out, :] = total[...]
     wait_bytes(gram_ref.at[pl.ds(0, 31 * strip), :], small.at[3])
     wait_bytes(staged.at[:, pl.ds(0, (writers - 1) * own)], send.at[0])
-    wait_bytes(other, send.at[1])
-    wait_bytes(pieces.at[pl.ds(0, 15)], send.at[2])
+    wait_bytes(pieces.at[pl.ds(0, 31)], send.at[2])
     wait_bytes(layers.at[pl.ds(0, 7)], send.at[3])
     wait_bytes(gram_ref.at[pl.ds(0, 31 * strip), :], send.at[4])
 
@@ -330,9 +319,7 @@
             pltpu.VMEM((snaps, own), F32),
             pltpu.VMEM((rows, cells), F32),
             pltpu.VMEM((snaps, snaps), F32),
-            pltpu.VMEM((snaps // 2, snaps), F32),
-            pltpu.VMEM((snaps // 2, snaps), F32),
-            pltpu.VMEM((16, snaps // 32, snaps), F32),
+            pltpu.VMEM((32, snaps // 32, snaps), F32),
             pltpu.VMEM((8, snaps // 32, snaps), F32),
             pltpu.VMEM((snaps // 32, snaps), F32),
             pltpu.SemaphoreType.DMA((5,)),

time: 90.6 us -> 88.6 us (0.978)
  Pallas kernels: 89.9 us -> 87.9 us
    pallas_call x1, Pallas kernels: 79.2 us -> 77.2 us  [regroup(): pl.pallas_call(functools.partial(regroup_kernel, chunks), out_shape=(*[ja...]
where the time goes in v4:
time: 88.6 us; the launch traced here: 88.5 us
  Pallas kernels  87.9 us (99%)
    pallas_call x1, Pallas kernels, regroup(): pl.pallas_call(functools.partial(regroup_kernel, chunks), out_shape=(*[ja...  77.2 us
    pallas_call x1, Pallas kernels, finish(): pl.pallas_call(functools.partial(finish_kernel, b, cw), out_shape=(jax.Sh...  10.7 us

profile of v4, /device:TPU:1, one launch (start us, length us, event | category | flops | bytes accessed | tf_op | source)
XLA Modules:
  0.0 88.5 jit_solution(3264253587261319852)
XLA Ops:
  0.6 77.2 %shard_map.30 = (bf16[256,4096]{1,0:T(8,128)(2,1)S(1)}, bf16[256,4096]{1,0:T(8,128)(2,1)S(1)}, bf16[256,4096]{1,0:T(8,128)(2,1)S(1)}, f32[256,256]{1,0:T(8,128)S(1)}) custom-call(f32[4,262144]{1,0:T(4,128)} %x_hbm.1), custom_call_target="tpu_custom_call" | custom-call | tf_op jit(solution)/shard_map/pallas_call | solution.py:313
  77.8 10.7 %shard_map.31 = (f32[256,4096]{1,0:T(8,128)}, f32[4,256]{1,0:T(4,128)}) custom-call(f32[256,256]{1,0:T(8,128)S(1)} %get-tuple-element.8.g_ref, bf16[256,4096]{1,0:T(8,128)(2,1)S(1)} %get-tuple-element.9.xh_ref, bf16[256,4096]{1,0:T(8,128)(2,1)S(1)} %get-tuple-element.10.xm_ref, bf16[256,4096]{1,0:T(8,128)(2,1)S(1)} %get-tuple-element.11.xl_ref), custom_call_target="tpu_custom_call" | custom-call | tf_op jit(solution)/shard_map/pallas_call | solution.py:117

commit v5 on v4

--- a/solution.py
+++ b/solution.py
@@ -11,7 +11,7 @@
 BF = jnp.bfloat16
 MESH = pl.DeviceIdType.MESH
 
-CHUNKS = ((0, 2560), (2560, 1024), (3584, 512))
+CHUNKS = ((0, 1920), (1920, 1152), (3072, 640), (3712, 384))
 
 def split3(v):
     hi=v.astype(BF); r=v-hi.astype(F32); mid=r.astype(BF); lo=(r-mid.astype(F32)).astype(BF)
@@ -112,7 +112,7 @@
         rows_out(p).wait()
 
 
-def finish(gram, x, b=64, cw=512):
+def finish(gram, x, b=64, cw=256):
     n, cells = x[0].shape
     return pl.pallas_call(
         functools.partial(finish_kernel, b, cw),

time: 88.6 us -> 88.9 us (level)
  no operation moved by 1% of the time
where the time goes in v5:
time: 88.9 us; the launch traced here: 88.8 us
  Pallas kernels  88.1 us (99%)
    pallas_call x1, Pallas kernels, regroup(): pl.pallas_call(functools.partial(regroup_kernel, chunks), out_shape=(*[ja...  77.5 us
    pallas_call x1, Pallas kernels, finish(): pl.pallas_call(functools.partial(finish_kernel, b, cw), out_shape=(jax.Sh...  10.6 us

profile of v5, /device:TPU:1, one launch (start us, length us, event | category | flops | bytes accessed | tf_op | source)
XLA Modules:
  0.0 88.8 jit_solution(9234034677276708240)
XLA Ops:
  0.6 77.5 %shard_map.30 = (bf16[256,4096]{1,0:T(8,128)(2,1)S(1)}, bf16[256,4096]{1,0:T(8,128)(2,1)S(1)}, bf16[256,4096]{1,0:T(8,128)(2,1)S(1)}, f32[256,256]{1,0:T(8,128)S(1)}) custom-call(f32[4,262144]{1,0:T(4,128)} %x_hbm.1), custom_call_target="tpu_custom_call" | custom-call | tf_op jit(solution)/shard_map/pallas_call | solution.py:313
  78.2 10.6 %shard_map.31 = (f32[256,4096]{1,0:T(8,128)}, f32[4,256]{1,0:T(4,128)}) custom-call(f32[256,256]{1,0:T(8,128)S(1)} %get-tuple-element.8.g_ref, bf16[256,4096]{1,0:T(8,128)(2,1)S(1)} %get-tuple-element.9.xh_ref, bf16[256,4096]{1,0:T(8,128)(2,1)S(1)} %get-tuple-element.10.xm_ref, bf16[256,4096]{1,0:T(8,128)(2,1)S(1)} %get-tuple-element.11.xl_ref), custom_call_target="tpu_custom_call" | custom-call | tf_op jit(solution)/shard_map/pallas_call | solution.py:117
